TPU v7x, 32 devices: a whole 2x2x4 slice. The times are simulated.
32 devices in a mesh: tm: 16 (over z, x, core), row: 2 (over y).
Axes of the slice: x: 2, y: 2, z: 4, core: 2. Of those that a mesh axis runs over, the one named last changes fastest.
Arguments:
- slice_ops: bfloat16 [16, 2048, 2048], P('tm', 'row'), may hold values from -6 to 6
- base_op: bfloat16 [2048, 2048], replicated, may hold values from -6 to 6
- load_table: float32 [16, 2048], replicated, may hold values from -1 to 1
- phase_idx: int32 [16, 2], P('tm'), may hold values from 0 to 15
- step_counts: int32 [16, 2], P('tm'), may hold values from 1 to 8
Outputs:
- windows: bfloat16 [16, 2048, 2048], P('tm', 'row')
All inputs are finite; a program needn't handle non-finite values.
Results may differ from a plain program's by a relative error of at most 0.012.
Values may be sent and summed in bfloat16 or wider, within the bound.
A program may use at most 128 MiB of HBM per device.

v0:
```python
import math

import jax
import jax.numpy as jnp
from jax import lax
from jax.sharding import PartitionSpec as P

LEVELS = 2


def shifted(value, axis, steps):
    count = lax.axis_size(axis)
    pairs = [(source, (source + steps) % count) for source in range(count)]
    return lax.ppermute(value, axis, pairs)


def shards(slice_ops, base_op, load_table, phase_idx, step_counts):
    state_size = base_op.shape[0]
    norm_scale = 1.0 / math.sqrt(state_size)
    phase_count = load_table.shape[0]
    index_row = phase_idx[0]
    count_row = step_counts[0].astype(jnp.float32)
    one_hot = (
        index_row[:, None] == lax.broadcasted_iota(jnp.int32, (index_row.shape[0], phase_count), 1)
    ).astype(jnp.float32)
    table_rows = jnp.dot(one_hot, load_table, precision=lax.Precision.HIGHEST)
    gain_rows = jnp.exp(0.1 * count_row[:, None] * table_rows)
    right_factor = (base_op * gain_rows[0]).astype(jnp.bfloat16)
    left_factor = (slice_ops[0] * gain_rows[1]).astype(jnp.bfloat16)
    product = jnp.dot(left_factor, right_factor, preferred_element_type=jnp.float32)
    current = (product * norm_scale).astype(jnp.bfloat16)
    for depth_level in range(LEVELS):
        distance = 2**depth_level
        whole = lax.all_gather(current, "row", axis=0, tiled=True)
        earlier = shifted(whole, "tm", distance)
        combined = jnp.dot(current, earlier, preferred_element_type=jnp.float32)
        current = (combined * norm_scale).astype(jnp.bfloat16)
    return current[None]


def solution(mesh):
    return jax.shard_map(
        shards,
        mesh=mesh,
        in_specs=(P("tm", "row", None), P(), P(), P("tm", None), P("tm", None)),
        out_specs=P("tm", "row", None),
        check_vma=False,
    )
```

profile of v0, /device:TPU:0, one launch (start us, length us, event | category | flops | bytes accessed | tf_op | source)
XLA Modules:
  0.0 542.5 jit_solution(17992595828902770426)
XLA Ops:
  6.5 0.0 copy-start
  6.5 0.0 all-gather.3.cloned.1.call-start
  6.5 0.7 multiply_bitcast_fusion
  7.2 0.2 copy-done
  7.5 0.9 fusion.7
  8.4 13.8 %multiply_convert_fusion.4 = bf16[1024,2048]{1,0:T(8,128)(2,1)} fusion(bf16[2048,2048]{1,0:T(8,128)(2,1)} %param.6, f32[2048]{0:T(1024)S(1)} %bitcast.19, bf16[1,1024,2048]{2,1,0:T(8,128)(2,1)} %param.5, f32[2048]{0:T(1024)S(1)} %bitcast.18), kind=kOutput, calls=%fused_computation.6 | convolution fusion | flops 8613003264 | bytes 16793600 | tf_op jit(solution)/shard_map/dot_general | solution.py:30
  22.2 0.0 all-gather.3.cloned.1.call-update
  22.2 0.0 all-gather.5.cloned.1.call-start
  22.3 106.8 %all-gather.3.cloned.1.call-done = bf16[2048,2048]{1,0:T(8,128)(2,1)} async-done(((bf16[1024,2048]{1,0:T(8,128)(2,1)}), bf16[2048,2048]{1,0:T(8,128)(2,1)}) %all-gather.3.cloned.1.call-update) | async-done | bytes 8388624 | tf_op jit(solution)/shard_map/all_gather | solution.py:34
  129.1 0.0 collective-permute-start
  129.1 95.8 %collective-permute-done = bf16[2048,2048]{1,0:T(8,128)(2,1)S(1)} collective-permute-done((bf16[2048,2048]{1,0:T(8,128)(2,1)}, bf16[2048,2048]{1,0:T(8,128)(2,1)S(1)}, u32[]{:S(2)}, u32[]{:S(2)}) %collective-permute-start) | collective-permute-done | bytes 8388640 | tf_op jit(solution)/shard_map/ppermute | solution.py:14
  224.9 12.1 %multiply_convert_fusion.3 = bf16[1024,2048]{1,0:T(8,128)(2,1)} fusion(bf16[1024,2048]{1,0:T(8,128)(2,1)} %multiply_convert_fusion.4, bf16[2048,2048]{1,0:T(8,128)(2,1)S(1)} %collective-permute-done), kind=kOutput, calls=%fused_computation.5 | convolution fusion | flops 8594128896 | bytes 16777216 | tf_op jit(solution)/shard_map/dot_general | solution.py:36
  237.0 0.0 all-gather.5.cloned.1.call-update
  237.0 101.5 %all-gather.5.cloned.1.call-done = bf16[2048,2048]{1,0:T(8,128)(2,1)} async-done(((bf16[1024,2048]{1,0:T(8,128)(2,1)}), bf16[2048,2048]{1,0:T(8,128)(2,1)}) %all-gather.5.cloned.1.call-update) | async-done | bytes 8388624 | tf_op jit(solution)/shard_map/all_gather | solution.py:34
  338.5 1.5 collective-permute-start.1
  340.0 183.6 %collective-permute-done.1 = bf16[2048,2048]{1,0:T(8,128)(2,1)S(1)} collective-permute-done((bf16[2048,2048]{1,0:T(8,128)(2,1)}, bf16[2048,2048]{1,0:T(8,128)(2,1)S(1)}, u32[]{:S(2)}, u32[]{:S(2)}) %collective-permute-start.1) | collective-permute-done | bytes 8388640 | tf_op jit(solution)/shard_map/ppermute | solution.py:14
  523.6 12.1 %fusion.6 = bf16[1,1024,2048]{2,1,0:T(8,128)(2,1)} fusion(bf16[1024,2048]{1,0:T(8,128)(2,1)} %multiply_convert_fusion.3, bf16[2048,2048]{1,0:T(8,128)(2,1)S(1)} %collective-permute-done.1), kind=kOutput, calls=%fused_computation.10 | convolution fusion | flops 8594128896 | bytes 16777216 | tf_op jit(solution)/shard_map/dot_general | solution.py:36
  (1 shorter events, 0.0 us)
Async XLA Ops:
  6.5 0.9 copy-start
  6.5 122.6 %all-gather.3.cloned.1.call-start = ((), (), s32[]{:S(2)}) async-start(), calls=%async_computation | async-start | bytes 12582912 | tf_op jit(solution)/shard_map/all_gather | solution.py:34
  22.2 316.3 %all-gather.5.cloned.1.call-start = ((), (), s32[]{:S(2)}) async-start(), calls=%async_computation.1 | async-start | bytes 12582912 | tf_op jit(solution)/shard_map/all_gather | solution.py:34
  129.1 95.8 %collective-permute-start = (bf16[2048,2048]{1,0:T(8,128)(2,1)}, bf16[2048,2048]{1,0:T(8,128)(2,1)S(1)}, u32[]{:S(2)}, u32[]{:S(2)}) collective-permute-start(bf16[2048,2048]{1,0:T(8,128)(2,1)} %all-gather.3.cloned.1.call-done), channel_id=1, source_target_pairs={{0,2},{2,4},{4,6},{6,8},{8,10},{10,12},{12,14},{14,16},{16,18},{18... | collective-permute-start | bytes 25165832 | tf_op jit(solution)/shard_map/ppermute | solution.py:14
  338.5 185.1 %collective-permute-start.1 = (bf16[2048,2048]{1,0:T(8,128)(2,1)}, bf16[2048,2048]{1,0:T(8,128)(2,1)S(1)}, u32[]{:S(2)}, u32[]{:S(2)}) collective-permute-start(bf16[2048,2048]{1,0:T(8,128)(2,1)} %all-gather.5.cloned.1.call-done), channel_id=1, source_target_pairs={{0,4},{2,6},{4,8},{6,10},{8,12},{10,14},{12,16},{14,18},{16,20},{1... | collective-permute-start | bytes 25165832 | tf_op jit(solution)/shard_map/ppermute | solution.py:14
Sparse Core Ops, SparseCore 0:
  22.3 106.6 all-gather.2
  237.1 101.3 all-gather.4
where the time goes:
time: 543 us
  waiting for transfers between devices  488 us (90%)
  matrix products  38.9 us (7%)
  between operations  13.4 us (2%)
    ppermute x2, waiting for transfers between devices, shifted(): return lax.ppermute(value, axis, pairs)  279 us
    all_gather x2, waiting for transfers between devices, shards(): whole = lax.all_gather(current, 'row', axis=0, tiled=True)  208 us
    dot_general x2, matrix products, shards(): combined = jnp.dot(current, earlier, preferred_element_type=jnp.float32)  24.2 us
    dot_general x1, matrix products, shards(): jnp.dot(left_factor, right_factor, preferred_element_type=jnp.float32)  13.8 us
  transfers between devices with their start and end apart: 4, of which 4 were waited for; matrix products, arithmetic and copies ran while one was open for 0% of the time, Pallas kernels for 0%

commit v1 on v0

v1 whole, which is shorter than its diff:
```python
import functools
import math

import jax
import jax.numpy as jnp
from jax import lax
from jax.experimental import pallas as pl
from jax.experimental.pallas import tpu as pltpu
from jax.sharding import PartitionSpec as P

MESH = pl.DeviceIdType.MESH
WIDTH = 256
TILE = 512
LAG = 2


def kernel(
    count, s_hbm, b_hbm, table, phase, steps, o_hbm,
    s, b, p, x, m1, m2, o, s_sem, b_sem, o_sem, send, r1o, r1c, r2o, r2c,
):
    rows, size = s.shape
    chunks = size // WIDTH
    norm = 1.0 / math.sqrt(size)
    k = lax.axis_index("tm")
    r = lax.axis_index("row")
    odd = lax.rem(k, 2)
    even = odd == 0
    own = pl.ds(pl.multiple_of(r * rows, rows), rows)
    cross = pl.ds(pl.multiple_of((1 - r) * rows, rows), rows)

    def cols(n):
        return pl.ds(pl.multiple_of(n * WIDTH, WIDTH), WIDTH)

    def load_b(n):
        return pltpu.make_async_copy(b_hbm.at[:, cols(n)], b.at[:, cols(n)], b_sem.at[n])

    def store_o(n):
        return pltpu.make_async_copy(o.at[:, cols(n)], o_hbm.at[0, :, cols(n)], o_sem.at[n])

    load_s = pltpu.make_async_copy(s_hbm.at[0], s, s_sem.at[0])
    load_s.start()
    for n in range(chunks):
        load_b(n).start()

    def wrap(index):
        return lax.rem(index + count, count)

    sibling = (k + 1, r)
    sibling_across = (k + 1, 1 - r)
    across = (k, 1 - r)
    next_one = (wrap(k + 1), r)
    next_two = (wrap(k + 3), r)

    barrier = pltpu.get_barrier_semaphore()

    def greet(*devices):
        for device in devices:
            pl.semaphore_signal(barrier, inc=1, device_id=device, device_id_type=MESH)

    @pl.when(even)
    def _():
        greet((wrap(k - 1), r), (wrap(k - 3), r), across)
        pl.semaphore_wait(barrier, 3)

    @pl.when(jnp.logical_not(even))
    def _():
        greet((k - 1, r), (k - 1, 1 - r))
        pl.semaphore_wait(barrier, 2)

    def remote(src, dst, kind, n, arrived, device):
        return pltpu.make_async_remote_copy(
            src_ref=src, dst_ref=dst, send_sem=send.at[kind, n], recv_sem=arrived.at[n],
            device_id=device, device_id_type=MESH,
        )

    def p_sibling(n):
        return remote(p.at[:, cols(n)], m1.at[own, cols(n)], 0, n, r1o, sibling)

    def p_across(n):
        return remote(p.at[:, cols(n)], m1.at[own, cols(n)], 1, n, r1c, sibling_across)

    def m1_own_sibling(n):
        return remote(m1.at[own, cols(n)], m2.at[own, cols(n)], 2, n, r2o, sibling)

    def m1_own_across(n):
        return remote(m1.at[own, cols(n)], m1.at[own, cols(n)], 3, n, r1c, across)

    def m1_cross_sibling(n):
        return remote(m1.at[cross, cols(n)], m2.at[cross, cols(n)], 4, n, r2c, sibling)

    def m2_own_across(n):
        return remote(m2.at[own, cols(n)], m2.at[own, cols(n)], 5, n, r2c, across)

    def p_next_two(n):
        return remote(p.at[:, cols(n)], m2.at[own, cols(n)], 0, n, r2o, next_two)

    def x_next_one(n):
        return remote(x.at[:, cols(n)], m1.at[own, cols(n)], 1, n, r1o, next_one)

    def landed(ref, part, n, arrived):
        remote(ref.at[part, cols(n)], ref.at[part, cols(n)], 0, n, arrived, across).wait_recv()

    def multiply(dst, left, right, n, scale):
        @pl.loop(0, rows // TILE)
        def _(t):
            at = pl.ds(pl.multiple_of(t * TILE, TILE), TILE)
            got = jnp.dot(left[at, :], right[:, cols(n)], preferred_element_type=jnp.float32)
            dst[at, cols(n)] = (got * scale).astype(jnp.bfloat16)

    def gain(j, at):
        row = table[pl.ds(phase[0, j], 1), at]
        return jnp.exp(0.1 * steps[0, j].astype(jnp.float32) * row)

    load_s.wait()
    gain_left = gain(1, slice(None))

    @pl.loop(0, rows // 64)
    def _(t):
        at = pl.ds(pl.multiple_of(t * 64, 64), 64)
        s[at, :] = (s[at, :].astype(jnp.float32) * gain_left).astype(jnp.bfloat16)

    @pl.loop(0, chunks)
    def _(n):
        load_b(n).wait()
        multiply(p, s, b, n, gain(0, cols(n)) * norm)

        @pl.when(even)
        def _():
            p_across(n).start()
            p_sibling(n).start()

        @pl.when(jnp.logical_not(even))
        def _():
            p_next_two(n).start()

    half = chunks // 2

    @pl.when(even)
    def _():
        def pass_m2(n):
            landed(m2, own, n, r2o)
            m2_own_across(n).start()

        @pl.loop(0, chunks + LAG)
        def _(n):
            @pl.when(n < chunks)
            def _():
                landed(m1, own, n, r1o)
                m1_own_across(n).start()
                m1_own_sibling(n).start()

            @pl.when(jnp.logical_and(lax.rem(n, 2) == 1, n < chunks))
            def _():
                pass_m2(n // 2)

            @pl.when(n >= LAG)
            def _():
                landed(m1, cross, n - LAG, r1c)
                m1_cross_sibling(n - LAG).start()
                multiply(x, p, m1, n - LAG, norm)

            @pl.when(n >= chunks)
            def _():
                pass_m2(half + n - chunks)

        @pl.loop(half + LAG, chunks)
        def _(n):
            pass_m2(n)

        @pl.loop(0, chunks)
        def _(n):
            landed(m2, cross, n, r2c)
            multiply(o, x, m2, n, norm)
            store_o(n).start()

        @pl.loop(0, chunks)
        def _(n):
            for copy in (p_sibling, p_across, m1_own_sibling, m1_own_across, m1_cross_sibling, m2_own_across):
                copy(n).wait_send()
            store_o(n).wait()

    @pl.when(jnp.logical_not(even))
    def _():
        @pl.loop(0, chunks)
        def _(n):
            landed(m1, own, n, r1o)
            landed(m1, cross, n, r1c)
            multiply(x, p, m1, n, norm)
            x_next_one(n).start()

        @pl.loop(0, chunks)
        def _(n):
            landed(m2, own, n, r2o)
            landed(m2, cross, n, r2c)
            multiply(o, x, m2, n, norm)
            store_o(n).start()

        @pl.loop(0, chunks)
        def _(n):
            for copy in (p_next_two, x_next_one):
                copy(n).wait_send()
            store_o(n).wait()


def shards(count, slice_ops, base_op, load_table, phase_idx, step_counts):
    _, rows, size = slice_ops.shape
    chunks = size // WIDTH
    bf16 = jnp.bfloat16
    dma = pltpu.SemaphoreType.DMA
    return pl.pallas_call(
        functools.partial(kernel, count),
        out_shape=jax.ShapeDtypeStruct(slice_ops.shape, bf16),
        in_specs=[
            pl.BlockSpec(memory_space=pl.ANY),
            pl.BlockSpec(memory_space=pl.ANY),
            pl.BlockSpec(memory_space=pltpu.VMEM),
            pl.BlockSpec(memory_space=pltpu.SMEM),
            pl.BlockSpec(memory_space=pltpu.SMEM),
        ],
        out_specs=pl.BlockSpec(memory_space=pl.ANY),
        scratch_shapes=[
            pltpu.VMEM((rows, size), bf16),
            pltpu.VMEM((size, size), bf16),
            pltpu.VMEM((rows, size), bf16),
            pltpu.VMEM((rows, size), bf16),
            pltpu.VMEM((size, size), bf16),
            pltpu.VMEM((size, size), bf16),
            pltpu.VMEM((rows, size), bf16),
            dma((1,)),
            dma((chunks,)),
            dma((chunks,)),
            dma((6, chunks)),
            dma((chunks,)),
            dma((chunks,)),
            dma((chunks,)),
            dma((chunks,)),
        ],
        compiler_params=pltpu.CompilerParams(
            collective_id=0, has_side_effects=True, vmem_limit_bytes=56 * 2**20
        ),
        cost_estimate=pl.CostEstimate(
            flops=6 * rows * size * size, bytes_accessed=2 * 4 * rows * size, transcendentals=0
        ),
    )(slice_ops, base_op, load_table, phase_idx, step_counts)


def solution(mesh):
    return jax.shard_map(
        functools.partial(shards, mesh.shape["tm"]),
        mesh=mesh,
        in_specs=(P("tm", "row", None), P(), P(), P("tm", None), P("tm", None)),
        out_specs=P("tm", "row", None),
        check_vma=False,
    )
```

time: 543 us -> 166 us (0.31)
  waiting for transfers between devices: 488 us -> 0 us
  Pallas kernels: 0 us -> 161 us
  matrix products: 38.9 us -> 0 us
  between operations: 13.4 us -> 0.01 us
    ppermute x2 -> x0, waiting for transfers between devices: 279 us -> none  [shifted(): return lax.ppermute(value, axis, pairs)]
    all_gather x2 -> x0, waiting for transfers between devices: 208 us -> none  [shards(): whole = lax.all_gather(current, 'row', axis=0, tiled=True)]
    pallas_call x0 -> x1, Pallas kernels: none -> 161 us  [shards(): pl.pallas_call(functools.partial(kernel, count), out_shape=jax.ShapeDtype...]
    dot_general x4 -> x0, matrix products: 38.9 us -> none  [the longest x2 24.2 us: shards(): combined = jnp.dot(current, earlier, preferred_element_type=jnp.float32)]
  transfers between devices with their start and end apart: 4 -> 0, of which waited for: 4 -> 0; matrix products, arithmetic and copies ran while one was open for 0% -> 0% of each run, Pallas kernels for 0% -> 0%
where the time goes in v1:
time: 166 us
  Pallas kernels  161 us (97%)
  local copies, waits for them, and re-layouts  4.79 us (3%)
    pallas_call x1, Pallas kernels, shards(): pl.pallas_call(functools.partial(kernel, count), out_shape=jax.ShapeDtype...  161 us
    unnamed x1, local copies, waits for them, and re-layouts  4.79 us

profile of v1, /device:TPU:0, one launch (start us, length us, event | category | flops | bytes accessed | tf_op | source)
XLA Modules:
  0.0 165.8 jit_solution(15919385435891265356)
XLA Ops:
  0.0 161.0 %shard_map.55 = bf16[1,1024,2048]{2,1,0:T(8,128)(2,1)} custom-call(bf16[1,1024,2048]{2,1,0:T(8,128)(2,1)} %s_hbm.1, bf16[2048,2048]{1,0:T(8,128)(2,1)} %b_hbm.1, f32[16,2048]{1,0:T(8,128)} %table.1, s32[1,2]{1,0:T(1,128)} %phase.1, s32[1,2]{1,0:T(1,128)} %steps.1), custom_call_target="tpu_custom_call" | custom-call | flops 25769803776 | bytes 16777216 | tf_op jit(solution)/shard_map/pallas_call | solution.py:210
  161.0 4.8 %copy.7 = bf16[1,1024,2048]{2,1,0:T(8,128)(2,1)} copy(bf16[1,1024,2048]{2,1,0:T(8,128)(2,1)} %shard_map.55) | data formatting | bytes 8388608

commit v2 on v1

--- a/solution.py
+++ b/solution.py
@@ -11,12 +11,12 @@
 MESH = pl.DeviceIdType.MESH
 WIDTH = 256
 TILE = 512
-LAG = 2
+SHARE = 1, 4
 
 
 def kernel(
     count, s_hbm, b_hbm, table, phase, steps, o_hbm,
-    s, b, p, x, m1, m2, o, s_sem, b_sem, o_sem, send, r1o, r1c, r2o, r2c,
+    s, b, p, x, m1, m2, o, q, y, s_sem, b_sem, o_sem, send, r1o, r1c, r2o, r2c, r1d, r2d, rq,
 ):
     rows, size = s.shape
     chunks = size // WIDTH
@@ -27,6 +27,11 @@
     even = odd == 0
     own = pl.ds(pl.multiple_of(r * rows, rows), rows)
     cross = pl.ds(pl.multiple_of((1 - r) * rows, rows), rows)
+    shared = q.shape[0]
+    rest = rows - shared
+    own_rest = pl.ds(pl.multiple_of(r * rows + shared, 128), rest)
+    cross_rest = pl.ds(pl.multiple_of((1 - r) * rows + shared, 128), rest)
+    cross_shared = pl.ds(pl.multiple_of((1 - r) * rows, rows), shared)
 
     def cols(n):
         return pl.ds(pl.multiple_of(n * WIDTH, WIDTH), WIDTH)
@@ -64,8 +69,8 @@
 
     @pl.when(jnp.logical_not(even))
     def _():
-        greet((k - 1, r), (k - 1, 1 - r))
-        pl.semaphore_wait(barrier, 2)
+        greet((k - 1, r), (k - 1, 1 - r), across)
+        pl.semaphore_wait(barrier, 3)
 
     def remote(src, dst, kind, n, arrived, device):
         return pltpu.make_async_remote_copy(
@@ -83,13 +88,13 @@
         return remote(m1.at[own, cols(n)], m2.at[own, cols(n)], 2, n, r2o, sibling)
 
     def m1_own_across(n):
-        return remote(m1.at[own, cols(n)], m1.at[own, cols(n)], 3, n, r1c, across)
+        return remote(m1.at[own_rest, cols(n)], m1.at[own_rest, cols(n)], 3, n, r1c, across)
 
     def m1_cross_sibling(n):
         return remote(m1.at[cross, cols(n)], m2.at[cross, cols(n)], 4, n, r2c, sibling)
 
     def m2_own_across(n):
-        return remote(m2.at[own, cols(n)], m2.at[own, cols(n)], 5, n, r2c, across)
+        return remote(m2.at[own_rest, cols(n)], m2.at[own_rest, cols(n)], 5, n, r2c, across)
 
     def p_next_two(n):
         return remote(p.at[:, cols(n)], m2.at[own, cols(n)], 0, n, r2o, next_two)
@@ -97,13 +102,22 @@
     def x_next_one(n):
         return remote(x.at[:, cols(n)], m1.at[own, cols(n)], 1, n, r1o, next_one)
 
+    def p_across_odd(n):
+        return remote(p.at[pl.ds(0, shared), cols(n)], q.at[:, cols(n)], 2, n, rq, across)
+
+    def q_next_two(n):
+        return remote(q.at[:, cols(n)], m2.at[cross_shared, cols(n)], 3, n, r2d, next_two)
+
+    def y_next_one(n):
+        return remote(y.at[:, cols(n)], m1.at[cross_shared, cols(n)], 4, n, r1d, next_one)
+
     def landed(ref, part, n, arrived):
         remote(ref.at[part, cols(n)], ref.at[part, cols(n)], 0, n, arrived, across).wait_recv()
 
-    def multiply(dst, left, right, n, scale):
-        @pl.loop(0, rows // TILE)
+    def multiply(dst, left, right, n, scale, tile=TILE):
+        @pl.loop(0, left.shape[0] // tile)
         def _(t):
-            at = pl.ds(pl.multiple_of(t * TILE, TILE), TILE)
+            at = pl.ds(pl.multiple_of(t * tile, tile), tile)
             got = jnp.dot(left[at, :], right[:, cols(n)], preferred_element_type=jnp.float32)
             dst[at, cols(n)] = (got * scale).astype(jnp.bfloat16)
 
@@ -131,6 +145,7 @@
 
         @pl.when(jnp.logical_not(even))
         def _():
+            p_across_odd(n).start()
             p_next_two(n).start()
 
     half = chunks // 2
@@ -141,35 +156,31 @@
             landed(m2, own, n, r2o)
             m2_own_across(n).start()
 
-        @pl.loop(0, chunks + LAG)
-        def _(n):
-            @pl.when(n < chunks)
-            def _():
-                landed(m1, own, n, r1o)
-                m1_own_across(n).start()
-                m1_own_sibling(n).start()
-
-            @pl.when(jnp.logical_and(lax.rem(n, 2) == 1, n < chunks))
+        @pl.loop(0, chunks)
+        def _(n):
+            landed(m1, own, n, r1o)
+            m1_own_across(n).start()
+            m1_own_sibling(n).start()
+
+            @pl.when(lax.rem(n, 2) == 1)
             def _():
                 pass_m2(n // 2)
 
-            @pl.when(n >= LAG)
-            def _():
-                landed(m1, cross, n - LAG, r1c)
-                m1_cross_sibling(n - LAG).start()
-                multiply(x, p, m1, n - LAG, norm)
-
-            @pl.when(n >= chunks)
-            def _():
-                pass_m2(half + n - chunks)
-
-        @pl.loop(half + LAG, chunks)
+        @pl.loop(half, chunks)
         def _(n):
             pass_m2(n)
 
         @pl.loop(0, chunks)
         def _(n):
-            landed(m2, cross, n, r2c)
+            landed(m1, cross_rest, n, r1c)
+            landed(m1, cross_shared, n, r1d)
+            m1_cross_sibling(n).start()
+            multiply(x, p, m1, n, norm)
+
+        @pl.loop(0, chunks)
+        def _(n):
+            landed(m2, cross_shared, n, r2d)
+            landed(m2, cross_rest, n, r2c)
             multiply(o, x, m2, n, norm)
             store_o(n).start()
 
@@ -187,6 +198,13 @@
             landed(m1, cross, n, r1c)
             multiply(x, p, m1, n, norm)
             x_next_one(n).start()
+            landed(q, slice(None), n, rq)
+            q_next_two(n).start()
+
+        @pl.loop(0, chunks)
+        def _(n):
+            multiply(y, q, m1, n, norm, shared)
+            y_next_one(n).start()
 
         @pl.loop(0, chunks)
         def _(n):
@@ -197,7 +215,7 @@
 
         @pl.loop(0, chunks)
         def _(n):
-            for copy in (p_next_two, x_next_one):
+            for copy in (p_next_two, x_next_one, p_across_odd, q_next_two, y_next_one):
                 copy(n).wait_send()
             store_o(n).wait()
 
@@ -205,6 +223,7 @@
 def shards(count, slice_ops, base_op, load_table, phase_idx, step_counts):
     _, rows, size = slice_ops.shape
     chunks = size // WIDTH
+    shared = rows * SHARE[0] // SHARE[1]
     bf16 = jnp.bfloat16
     dma = pltpu.SemaphoreType.DMA
     return pl.pallas_call(
@@ -226,10 +245,15 @@
             pltpu.VMEM((size, size), bf16),
             pltpu.VMEM((size, size), bf16),
             pltpu.VMEM((rows, size), bf16),
+            pltpu.VMEM((shared, size), bf16),
+            pltpu.VMEM((shared, size), bf16),
             dma((1,)),
             dma((chunks,)),
             dma((chunks,)),
             dma((6, chunks)),
+            dma((chunks,)),
+            dma((chunks,)),
+            dma((chunks,)),
             dma((chunks,)),
             dma((chunks,)),
             dma((chunks,)),

time: 166 us -> 151 us (0.910)
  Pallas kernels: 161 us -> 146 us
    pallas_call x1, Pallas kernels: 161 us -> 146 us  [shards(): pl.pallas_call(functools.partial(kernel, count), out_shape=jax.ShapeDtype...]
where the time goes in v2:
time: 151 us
  Pallas kernels  146 us (97%)
  local copies, waits for them, and re-layouts  4.79 us (3%)
    pallas_call x1, Pallas kernels, shards(): pl.pallas_call(functools.partial(kernel, count), out_shape=jax.ShapeDtype...  146 us
    unnamed x1, local copies, waits for them, and re-layouts  4.79 us

profile of v2, /device:TPU:0, one launch (start us, length us, event | category | flops | bytes accessed | tf_op | source)
XLA Modules:
  0.0 150.6 jit_solution(8876114375290148898)
XLA Ops:
  0.0 145.8 %shard_map.55 = bf16[1,1024,2048]{2,1,0:T(8,128)(2,1)} custom-call(bf16[1,1024,2048]{2,1,0:T(8,128)(2,1)} %s_hbm.1, bf16[2048,2048]{1,0:T(8,128)(2,1)} %b_hbm.1, f32[16,2048]{1,0:T(8,128)} %table.1, s32[1,2]{1,0:T(1,128)} %phase.1, s32[1,2]{1,0:T(1,128)} %steps.1), custom_call_target="tpu_custom_call" | custom-call | flops 25769803776 | bytes 16777216 | tf_op jit(solution)/shard_map/pallas_call | solution.py:229
  145.8 4.8 %copy.7 = bf16[1,1024,2048]{2,1,0:T(8,128)(2,1)} copy(bf16[1,1024,2048]{2,1,0:T(8,128)(2,1)} %shard_map.55) | data formatting | bytes 8388608

commit v3 on v2

--- a/solution.py
+++ b/solution.py
@@ -198,13 +198,16 @@
             landed(m1, cross, n, r1c)
             multiply(x, p, m1, n, norm)
             x_next_one(n).start()
+
+        @pl.loop(0, chunks)
+        def _(n):
             landed(q, slice(None), n, rq)
-            q_next_two(n).start()
 
         @pl.loop(0, chunks)
         def _(n):
             multiply(y, q, m1, n, norm, shared)
             y_next_one(n).start()
+            q_next_two(n).start()
 
         @pl.loop(0, chunks)
         def _(n):

time: 151 us -> 146 us (0.967)
  Pallas kernels: 146 us -> 141 us
    pallas_call x1, Pallas kernels: 146 us -> 141 us  [shards(): pl.pallas_call(functools.partial(kernel, count), out_shape=jax.ShapeDtype...]
where the time goes in v3:
time: 146 us; the launch traced here: 145 us
  Pallas kernels  141 us (97%)
  local copies, waits for them, and re-layouts  4.79 us (3%)
    pallas_call x1, Pallas kernels, shards(): pl.pallas_call(functools.partial(kernel, count), out_shape=jax.ShapeDtype...  141 us
    unnamed x1, local copies, waits for them, and re-layouts  4.79 us

profile of v3, /device:TPU:0, one launch (start us, length us, event | category | flops | bytes accessed | tf_op | source)
XLA Modules:
  0.0 145.4 jit_solution(4410447079764418067)
XLA Ops:
  0.0 140.6 %shard_map.55 = bf16[1,1024,2048]{2,1,0:T(8,128)(2,1)} custom-call(bf16[1,1024,2048]{2,1,0:T(8,128)(2,1)} %s_hbm.1, bf16[2048,2048]{1,0:T(8,128)(2,1)} %b_hbm.1, f32[16,2048]{1,0:T(8,128)} %table.1, s32[1,2]{1,0:T(1,128)} %phase.1, s32[1,2]{1,0:T(1,128)} %steps.1), custom_call_target="tpu_custom_call" | custom-call | flops 25769803776 | bytes 16777216 | tf_op jit(solution)/shard_map/pallas_call | solution.py:232
  140.6 4.8 %copy.7 = bf16[1,1024,2048]{2,1,0:T(8,128)(2,1)} copy(bf16[1,1024,2048]{2,1,0:T(8,128)(2,1)} %shard_map.55) | data formatting | bytes 8388608

commit v4 on v3

--- a/solution.py
+++ b/solution.py
@@ -42,8 +42,14 @@
     def store_o(n):
         return pltpu.make_async_copy(o.at[:, cols(n)], o_hbm.at[0, :, cols(n)], o_sem.at[n])
 
-    load_s = pltpu.make_async_copy(s_hbm.at[0], s, s_sem.at[0])
-    load_s.start()
+    quarter = rows // 4
+
+    def load_s(n):
+        at = pl.ds(pl.multiple_of(n * quarter, quarter), quarter)
+        return pltpu.make_async_copy(s_hbm.at[0, at], s.at[at], s_sem.at[n])
+
+    for n in range(4):
+        load_s(n).start()
     for n in range(chunks):
         load_b(n).start()
 
@@ -125,12 +131,12 @@
         row = table[pl.ds(phase[0, j], 1), at]
         return jnp.exp(0.1 * steps[0, j].astype(jnp.float32) * row)
 
-    load_s.wait()
     gain_left = gain(1, slice(None))
 
-    @pl.loop(0, rows // 64)
+    @pl.loop(0, 4)
     def _(t):
-        at = pl.ds(pl.multiple_of(t * 64, 64), 64)
+        load_s(t).wait()
+        at = pl.ds(pl.multiple_of(t * quarter, quarter), quarter)
         s[at, :] = (s[at, :].astype(jnp.float32) * gain_left).astype(jnp.bfloat16)
 
     @pl.loop(0, chunks)
@@ -250,7 +256,7 @@
             pltpu.VMEM((rows, size), bf16),
             pltpu.VMEM((shared, size), bf16),
             pltpu.VMEM((shared, size), bf16),
-            dma((1,)),
+            dma((4,)),
             dma((chunks,)),
             dma((chunks,)),
             dma((6, chunks)),

time: 146 us -> 145 us (level)
  no operation moved by 1% of the time
where the time goes in v4:
time: 145 us
  Pallas kernels  140 us (97%)
  local copies, waits for them, and re-layouts  4.79 us (3%)
    pallas_call x1, Pallas kernels, shards(): pl.pallas_call(functools.partial(kernel, count), out_shape=jax.ShapeDtype...  140 us
    unnamed x1, local copies, waits for them, and re-layouts  4.79 us

profile of v4, /device:TPU:0, one launch (start us, length us, event | category | flops | bytes accessed | tf_op | source)
XLA Modules:
  0.0 144.7 jit_solution(1220205143231197094)
XLA Ops:
  0.0 139.9 %shard_map.55 = bf16[1,1024,2048]{2,1,0:T(8,128)(2,1)} custom-call(bf16[1,1024,2048]{2,1,0:T(8,128)(2,1)} %s_hbm.1, bf16[2048,2048]{1,0:T(8,128)(2,1)} %b_hbm.1, f32[16,2048]{1,0:T(8,128)} %table.1, s32[1,2]{1,0:T(1,128)} %phase.1, s32[1,2]{1,0:T(1,128)} %steps.1), custom_call_target="tpu_custom_call" | custom-call | flops 25769803776 | bytes 16777216 | tf_op jit(solution)/shard_map/pallas_call | solution.py:238
  139.9 4.8 %copy.7 = bf16[1,1024,2048]{2,1,0:T(8,128)(2,1)} copy(bf16[1,1024,2048]{2,1,0:T(8,128)(2,1)} %shard_map.55) | data formatting | bytes 8388608
